TPU v7x, 128 devices: a whole 4x4x4 slice. The times are simulated.
128 devices in a mesh: dp: 8 (over z, x_hi), ctx: 16 (over x_lo, y, core).
Axes of the slice: x: 4 (x_hi: 2, x_lo: 2; x = x_hi * 2 + x_lo), y: 4, z: 4, core: 2. Of those that a mesh axis runs over, the one named last changes fastest.
Arguments:
- hidden: bfloat16 [65536, 4096], P(('dp', 'ctx')), parts along dimension 0, may hold values from -24 to 24
- dest: int32 [65536], P(('dp', 'ctx')), parts along dimension 0, may hold values from 0 to 8191, as said below
- doc_ids: int32 [65536], P('dp'), parts along dimension 0, may hold values from 0 to 63, never falling along the last dimension, each value on 1 to 1024 neighbouring positions
- w_query: bfloat16 [4096, 2048], P('ctx'), may hold values from -0.09375 to 0.09375
- key_weight: bfloat16 [4096, 512], P('ctx'), may hold values from -0.09375 to 0.09375
- value_weight: bfloat16 [4096, 512], P('ctx'), may hold values from -0.09375 to 0.09375
Outputs:
- attended: bfloat16 [65536, 2048], P(('dp', 'ctx')), parts along dimension 0
There are 8 independent parts, one for each index of `dp`. A program takes and returns all parts, laid end to end along the dimension named above; an argument that names none is the same for every part. Nothing has to cross between parts.
Inputs may be any that keep to these rules, and one draw needn't show every extreme that they name: `dest`: A permutation. Each block of 512 loader rows sends at most 64 rows to one block of 512 context positions, exactly 64 to some.
All inputs are finite; a program needn't handle non-finite values.
Results may differ from a plain program's by a relative error of at most 0.024.
Values may be sent and summed in bfloat16 or wider, within the bound.
A program may use at most 128 MiB of HBM per device.

v0:
```python
import functools

import jax
import jax.numpy as jnp
from jax import lax
from jax.experimental import pallas as pl
from jax.experimental.pallas import tpu as pltpu
from jax.sharding import PartitionSpec as P

HEAD = 128
BLOCK = 512
CHIPS = 8
CHUNKS = 6
WIDE = 256
SLOTS = 256
WINDOW = 640
MESH = pl.DeviceIdType.MESH
rope_base = 500000.0 * 16.0 ** (128.0 / 126.0)
SCORE = HEAD**-0.5 * 1.4426950408889634
F32, BF16 = jnp.float32, jnp.bfloat16


def kernel(
    hid, dest, docs, cos, sin, wq, wk, wv, out,
    x_all, w_all, dests, pack, unpack, meta_s, meta_r, qkv, snd, rcv, keys, vals, qs, outs, bias,
    one, six,
):
    dp, cx = lax.axis_index("dp"), lax.axis_index("ctx")
    z, xh = dp // 2, lax.rem(dp, 2)
    xl, y, core = cx // 8, lax.rem(cx // 2, 4), lax.rem(cx, 2)
    chip, half = cx // 2, lax.rem(z, 2)
    other = 1 - core

    def at_y(step):
        return lax.rem(y + step, 4)

    sibling = (dp, chip * 2 + other)
    inner = (dp, (1 - xl) * 8 + y * 2 + core)
    outer = (z * 2 + 1 - xh, (1 - xl) * 8 + y * 2 + core)
    above = (lax.rem(z + 1, 4) * 2 + xh, cx)
    below = (lax.rem(z + 3, 4) * 2 + xh, cx)

    def peer(step):
        return lax.rem(chip + step, CHIPS)

    (hid_l, hid_s, hid_r, dst_s, dst_r, met_s, met_r) = (one.at[i] for i in range(7))
    (w_l, w_s, w_r, y_s, y_r, x_s, x_r, z_s, z_r, a_s, a_r, h_s, h_r, o_l, o_s, o_r) = (
        six.at[i] for i in range(16)
    )

    barrier = pltpu.get_barrier_semaphore()
    near = [sibling, outer, above, below] + [(dp, peer(r) * 2 + core) for r in range(1, CHIPS)]
    for device in near:
        pl.semaphore_signal(barrier, inc=1, device_id=device, device_id_type=MESH)
    pl.semaphore_wait(barrier, len(near))

    def remote(src, dst, s, r, device):
        return pltpu.make_async_remote_copy(
            src_ref=src, dst_ref=dst, send_sem=s, recv_sem=r, device_id=device, device_id_type=MESH
        )

    def drain(ref, sem):
        pltpu.make_async_copy(ref, ref, sem).wait()

    def columns(k, of):
        if k == 0:
            return wk.at[:, pl.ds(pl.multiple_of(of * WIDE, WIDE), WIDE)]
        if k == 1:
            return wv.at[:, pl.ds(pl.multiple_of(of * WIDE, WIDE), WIDE)]
        return wq.at[:, pl.ds(pl.multiple_of(of * 1024 + (k - 2) * WIDE, WIDE), WIDE)]

    mine = pl.ds(pl.multiple_of(core * 256, 256), 256)
    my_rows = pl.ds(pl.multiple_of(core * BLOCK, BLOCK), BLOCK)
    for k in range(CHUNKS):
        spot = w_all.at[k, chip, mine]
        remote(columns(k, other), spot, w_s.at[k], w_r.at[k], sibling).start()
        pltpu.make_async_copy(columns(k, core), spot, w_l.at[k]).start()
    dests[core] = jnp.broadcast_to(dest[...], (8, BLOCK))
    remote(dests.at[core], dests.at[core], dst_s, dst_r, sibling).start()
    remote(hid, x_all.at[my_rows], hid_s, hid_r, sibling).start()
    pltpu.make_async_copy(hid, x_all.at[my_rows], hid_l).start()

    sent_half = pl.ds(pl.multiple_of(half * 256, 256), 256)
    low = pl.ds(pl.multiple_of(half * 256, 128), 128)
    high = pl.ds(pl.multiple_of(half * 256 + 128, 128), 128)

    def stage_y(k):
        own = w_all.at[k, chip, mine]
        drain(own, w_l.at[k])
        drain(own, w_r.at[k])
        spot = w_all.at[k, chip, sent_half]
        for step in (1, 3, 2):
            remote(spot, spot, y_s.at[k], y_r.at[k], (dp, xl * 8 + at_y(step) * 2 + core)).start()
        remote(spot, spot, x_s.at[k], x_r.at[k], inner).start()

    def to_z(k, shard):
        spot = w_all.at[k, shard, low]
        remote(spot, spot, z_s.at[k], z_r.at[k], below).start()
        spot = w_all.at[k, shard, high]
        remote(spot, spot, z_s.at[k], z_r.at[k], above).start()

    def pieces(k, n):
        return w_all.at[k, pl.ds(0, n), pl.ds(0, 256)]

    def stage_x(k):
        drain(pieces(k, 3), y_r.at[k])
        for step in (1, 3, 2):
            spot = w_all.at[k, xl * 4 + at_y(step), sent_half]
            remote(spot, spot, x_s.at[k], x_r.at[k], outer).start()
        for step in (1, 3, 2):
            to_z(k, xl * 4 + at_y(step))

    def stage_z(k):
        drain(pieces(k, 4), x_r.at[k])
        for step in range(4):
            to_z(k, (1 - xl) * 4 + at_y(step))

    def project(k):
        drain(pieces(k, 7), z_r.at[k])

        def rows(m, _):
            at = pl.ds(pl.multiple_of(m * 512, 512), 512)
            qkv[at, :] = jnp.dot(
                x_all[at, :], w_all[k].reshape(CHIPS * 512, WIDE), preferred_element_type=F32
            ).astype(BF16)
            return 0

        lax.fori_loop(0, 2, rows, 0)

        def send(r, _):
            j = peer(r)
            snd[k, j] = jnp.dot(
                pack[pl.ds(pl.multiple_of(j * SLOTS, SLOTS), SLOTS), :], qkv[...],
                preferred_element_type=F32,
            ).astype(BF16)
            remote(
                snd.at[k, j], rcv.at[k, chip], a_s.at[k], a_r.at[k], (dp, j * 2 + core)
            ).start()
            return 0

        lax.fori_loop(1, CHIPS, send, 0)
        rcv[k, chip] = jnp.dot(
            pack[pl.ds(pl.multiple_of(chip * SLOTS, SLOTS), SLOTS), :], qkv[...],
            preferred_element_type=F32,
        ).astype(BF16)

    def placed(k, t):
        got = rcv[k, :, pl.ds(pl.multiple_of(t * 128, 128), 128), :].reshape(CHIPS * 128, WIDE)
        return jnp.dot(unpack[t], got, preferred_element_type=F32)

    def turned(v, t):
        at = pl.ds(pl.multiple_of(t * BLOCK, BLOCK), BLOCK)
        return (v * cos[at, :] + pltpu.roll(v, 64, 1) * sin[at, :]).astype(BF16)

    following = (dp, peer(1) * 2 + core)

    def halo(ref, i):
        remote(
            ref.at[:, pl.ds(1024, 512)], ref.at[:, pl.ds(0, 512)], h_s.at[i], h_r.at[i], following
        ).start()

    def receive(k):
        drain(rcv.at[k, pl.ds(0, 7)], a_r.at[k])

        def block(t, _):
            v = placed(k, t)
            for h in range(2):
                head = v[:, h * HEAD : (h + 1) * HEAD]

                @pl.when(k == 0)
                def _():
                    keys[h, pl.ds(pl.multiple_of(512 + t * 512, 512), 512), :] = turned(head, t)

                @pl.when(k == 1)
                def _():
                    vals[h, pl.ds(pl.multiple_of(512 + t * 512, 512), 512), :] = head.astype(BF16)

                @pl.when(k >= 2)
                def _():
                    qs[h, pl.ds(pl.multiple_of(t * 512, 512), 512), :] = turned(head, t)

            return 0

        lax.fori_loop(0, 2, block, 0)

        @pl.when(k == 0)
        def _():
            halo(keys, 0)

        @pl.when(k == 1)
        def _():
            halo(vals, 1)

        @pl.when(k == 2)
        def _():
            drain(keys.at[:, pl.ds(0, 512)], h_r.at[0])
            drain(vals.at[:, pl.ds(0, 512)], h_r.at[1])

        @pl.when(k >= 2)
        def _():
            attend(k - 2)

    def attend(c):
        g = c // 2

        def tile(i, _):
            at = pl.multiple_of(i * 128, 128)
            q = qs[:, pl.ds(at, 128), :].reshape(256, HEAD)
            s = lax.dot_general(
                q, keys[g, pl.ds(at, WINDOW), :], (((1,), (1,)), ((), ())),
                preferred_element_type=F32,
            )
            s = s.reshape(2, 128, WINDOW) * SCORE + bias[i][None]
            s = s.reshape(256, WINDOW)
            e = jnp.exp2(s - jnp.max(s, axis=1, keepdims=True))
            total = jnp.sum(e, axis=1, keepdims=True)
            o = jnp.dot(e.astype(BF16), vals[g, pl.ds(at, WINDOW), :], preferred_element_type=F32)
            o = (o / total).astype(BF16)
            to = pl.ds(pl.multiple_of(lax.rem(i, 4) * 128, 128), 128)
            outs[i // 4, c, to, pl.ds(0, HEAD)] = o[:128]
            outs[i // 4, c, to, pl.ds(HEAD, HEAD)] = o[128:]
            return 0

        lax.fori_loop(0, 8, tile, 0)
        spot = out.at[:, pl.ds(pl.multiple_of(core * 1024 + c * WIDE, WIDE), WIDE)]
        remote(outs.at[other, c], spot, o_s.at[c], o_r.at[c], sibling).start()
        pltpu.make_async_copy(outs.at[core, c], spot, o_l.at[c]).start()

    stage_y(0)
    stage_y(1)

    drain(dests.at[core], dst_r)
    tri = (
        lax.broadcasted_iota(jnp.int32, (BLOCK, BLOCK), 0)
        <= lax.broadcasted_iota(jnp.int32, (BLOCK, BLOCK), 1)
    ).astype(BF16)
    targets = jnp.zeros((8, CHIPS * SLOTS), F32)
    for b in range(2):
        d = dests[b][:1]
        owner = lax.shift_right_logical(d, 9)
        hits = lax.broadcasted_iota(jnp.int32, (16, BLOCK), 0) == owner
        counts = jnp.dot(hits.astype(BF16), tri, preferred_element_type=F32)
        rank = jnp.sum(jnp.where(hits, counts, 0.0), axis=0, keepdims=True) - 1.0
        slot = (owner * 2 + b) * 64 + rank.astype(jnp.int32)

        def fill(m, _):
            at = pl.multiple_of(m * 256, 256)
            pack[pl.ds(at, 256), pl.ds(b * BLOCK, BLOCK)] = (
                lax.broadcasted_iota(jnp.int32, (256, BLOCK), 0) + at == slot
            ).astype(BF16)
            return 0

        lax.fori_loop(0, 8, fill, 0)
        target = jnp.bitwise_and(d, 511) + 1
        row = lax.broadcasted_iota(jnp.int32, (8, BLOCK), 0)
        digits = jnp.where(
            row == 0,
            lax.shift_right_logical(target, 5),
            jnp.where(row == 1, jnp.bitwise_and(target, 31), 0),
        )
        targets = targets + lax.dot_general(
            digits.astype(F32).astype(BF16), pack[:, b * BLOCK : (b + 1) * BLOCK],
            (((1,), (1,)), ((), ())), preferred_element_type=F32,
        )
    targets = targets[:1] * 32.0 + targets[1:2]
    for j in range(CHIPS):
        for t in range(2):
            at = (j * 2 + t) * 128
            meta_s[j, t : t + 1, :] = targets[:, at : at + 128]
        meta_s[j, 2:8, :] = jnp.zeros((6, 128), F32)
    for r in range(1, CHIPS):
        j = peer(r)
        remote(meta_s.at[j], meta_r.at[chip], met_s, met_r, (dp, j * 2 + core)).start()
    meta_r[chip] = meta_s[chip]

    stage_x(0)

    def mask(i, _):
        at = pl.multiple_of(i * 128, 128)
        own = docs[:, pl.ds(pl.multiple_of(at + 512, 128), 128)].astype(F32)
        own = jnp.transpose(jnp.broadcast_to(own, (128, 128)))[:, :1]
        row = lax.broadcasted_iota(jnp.int32, (128, WINDOW), 0)
        col = lax.broadcasted_iota(jnp.int32, (128, WINDOW), 1)
        seen = (col > row) & (col <= row + 512)
        seen = seen & (own == docs[:, pl.ds(at, WINDOW)].astype(F32))
        bias[i] = jnp.where(seen, 0.0, -1e30)
        return 0

    lax.fori_loop(0, 8, mask, 0)

    stage_y(2)
    stage_x(1)
    stage_z(0)

    drain(meta_r.at[pl.ds(0, 7)], met_r)
    place = lax.broadcasted_iota(jnp.int32, (BLOCK, 128), 0).astype(F32) + 1.0
    for t in range(2):
        for i in range(CHIPS):
            unpack[t, :, i * 128 : (i + 1) * 128] = (place == meta_r[i, t : t + 1, :]).astype(BF16)

    drain(x_all.at[my_rows], hid_l)
    drain(x_all.at[my_rows], hid_r)

    def step(i, _):
        @pl.when(i < CHUNKS - 3)
        def _():
            stage_y(i + 3)

        @pl.when(i < CHUNKS - 2)
        def _():
            stage_x(i + 2)

        @pl.when(i < CHUNKS - 1)
        def _():
            stage_z(i + 1)

        @pl.when(i < CHUNKS)
        def _():
            project(i)

        @pl.when(i >= 1)
        def _():
            receive(i - 1)

        return 0

    lax.fori_loop(0, CHUNKS + 1, step, 0)

    for c in range(4):
        spot = out.at[:, pl.ds(c * WIDE, WIDE)]
        drain(spot, o_l.at[c])
        drain(spot, o_r.at[c])
        drain(outs.at[0, c], o_s.at[c])
    for k in range(CHUNKS):
        drain(pieces(k, 1), w_s.at[k])
        drain(pieces(k, 3), y_s.at[k])
        drain(pieces(k, 4), x_s.at[k])
        drain(pieces(k, 7), z_s.at[k])
        drain(snd.at[k, pl.ds(0, 7)], a_s.at[k])
    drain(keys.at[:, pl.ds(0, 512)], h_s.at[0])
    drain(vals.at[:, pl.ds(0, 512)], h_s.at[1])
    drain(x_all.at[my_rows], hid_s)
    drain(dests.at[core], dst_s)
    drain(meta_s.at[pl.ds(0, 7)], met_s)


def on_device(hidden, dest, doc_ids, w_query, key_weight, value_weight):
    chip = lax.axis_index("ctx") // 2
    positions = (chip * 1024 + jnp.arange(1024, dtype=jnp.int32)).astype(F32)
    freq = jnp.arange(HEAD // 2, dtype=F32)
    inverse = jnp.exp(-(2.0 * freq / HEAD) * jnp.log(F32(rope_base)))
    angles = positions[:, None] * inverse[None, :]
    cosine, sine = jnp.cos(angles), jnp.sin(angles)
    cosine = jnp.concatenate([cosine, cosine], axis=1)
    sine = jnp.concatenate([-sine, sine], axis=1)
    docs = jnp.concatenate([jnp.full((BLOCK,), -1, jnp.int32), doc_ids])
    docs = lax.dynamic_slice_in_dim(docs, chip * 1024, 1536, 0).reshape(1, 1536)
    anywhere = pl.BlockSpec(memory_space=pl.ANY)
    local = pl.BlockSpec(memory_space=pltpu.VMEM)
    return pl.pallas_call(
        kernel,
        out_shape=jax.ShapeDtypeStruct((BLOCK, 2048), BF16),
        in_specs=[anywhere, local, local, local, local, anywhere, anywhere, anywhere],
        out_specs=anywhere,
        scratch_shapes=[
            pltpu.VMEM((1024, 4096), BF16),
            pltpu.VMEM((CHUNKS, CHIPS, 512, WIDE), BF16),
            pltpu.VMEM((2, 8, BLOCK), jnp.int32),
            pltpu.VMEM((CHIPS * SLOTS, 1024), BF16),
            pltpu.VMEM((2, BLOCK, 1024), BF16),
            pltpu.VMEM((CHIPS, 8, 128), F32),
            pltpu.VMEM((CHIPS, 8, 128), F32),
            pltpu.VMEM((1024, WIDE), BF16),
            pltpu.VMEM((CHUNKS, CHIPS, SLOTS, WIDE), BF16),
            pltpu.VMEM((CHUNKS, CHIPS, SLOTS, WIDE), BF16),
            pltpu.VMEM((2, 1536, HEAD), BF16),
            pltpu.VMEM((2, 1536, HEAD), BF16),
            pltpu.VMEM((2, 1024, HEAD), BF16),
            pltpu.VMEM((2, 4, BLOCK, WIDE), BF16),
            pltpu.VMEM((8, 128, WINDOW), F32),
            pltpu.SemaphoreType.DMA((7,)),
            pltpu.SemaphoreType.DMA((16, CHUNKS)),
        ],
        compiler_params=pltpu.CompilerParams(
            collective_id=0, has_side_effects=True, vmem_limit_bytes=60 * 2**20
        ),
    )(hidden, dest.reshape(1, BLOCK), docs, cosine, sine, w_query, key_weight, value_weight)


def solution(mesh):
    placed = (
        P(("dp", "ctx"), None),
        P(("dp", "ctx")),
        P("dp"),
        P("ctx", None),
        P("ctx", None),
        P("ctx", None),
    )
    return jax.shard_map(
        on_device, mesh=mesh, in_specs=placed, out_specs=P(("dp", "ctx"), None), check_vma=False
    )
```

profile of v0, /device:TPU:123, one launch (start us, length us, event | category | flops | bytes accessed | tf_op | source)
XLA Modules:
  0.0 159.9 jit_solution(10940768890796914500)
XLA Ops:
  0.0 0.8 pad_dynamic-slice_fusion
  0.8 0.6 reshape.19.docs
  1.4 1.9 %fusion = (f32[1024,64]{1,0:T(8,128)S(1)}, f32[1024,64]{1,0:T(8,128)S(1)}, f32[1024,64]{1,0:T(8,128)S(1)}) fusion(f32[64]{0:T(128)S(1)} %multiply_exponential_fusion, f32[1024]{0:T(1024)S(1)} %add_convert_fusion), kind=kLoop, calls=%fused_computation.4 | loop fusion | flops 131072 | bytes 790784 | tf_op jit(solution)/shard_map/neg | solution.py:355
  3.3 1.3 pad_maximum_fusion
  4.6 152.1 %shard_map.64 = bf16[512,2048]{1,0:T(8,128)(2,1)} custom-call(bf16[512,4096]{1,0:T(8,128)(2,1)} %hid.1, s32[1,512]{1,0:T(1,128)} %bitcast.1, s32[1,1536]{1,0:T(1,128)} %reshape.19.docs, f32[1024,128]{1,0:T(8,128)} %get-tuple-element.8.cos, f32[1024,128]{1,0:T(8,128)} %get-tuple-element.9.sin, bf16[256,2048]{1,0:T(8,128)(2,1)} %wq.1, bf16[256,512]{1,0:T(8,128)(2,1)} %wk.1, ...), custom_call_target="tpu_custom_call" | custom-call | tf_op jit(solution)/shard_map/pallas_call | solution.py:360
  156.8 3.2 %copy.8 = bf16[512,2048]{1,0:T(8,128)(2,1)} copy(bf16[512,2048]{1,0:T(8,128)(2,1)} %shard_map.64) | data formatting | bytes 4194304
  (2 shorter events, 0.0 us)
where the time goes:
time: 160 us
  Pallas kernels  152 us (95%)
  local copies, waits for them, and re-layouts  4.54 us (3%)
  other arithmetic  3.22 us (2%)
    pallas_call x1, Pallas kernels, on_device(): pl.pallas_call(kernel, out_shape=jax.ShapeDtypeStruct((BLOCK, 2048), BF16...  152 us

commit v1 on v0

--- a/solution.py
+++ b/solution.py
@@ -1,7 +1,6 @@
-import functools
-
 import jax
 import jax.numpy as jnp
+import numpy as np
 from jax import lax
 from jax.experimental import pallas as pl
 from jax.experimental.pallas import tpu as pltpu
@@ -18,11 +17,22 @@
 rope_base = 500000.0 * 16.0 ** (128.0 / 126.0)
 SCORE = HEAD**-0.5 * 1.4426950408889634
 F32, BF16 = jnp.float32, jnp.bfloat16
+QUARTERS = (False, False, True, True, True, True)
+
+
+def angles():
+    inverse = rope_base ** (-2.0 * np.arange(64) / HEAD)
+    steps = [np.arange(8) * 1024, np.arange(32) * 32, np.arange(32)]
+    parts = []
+    for at in steps:
+        angle = at[:, None] * inverse[None, :]
+        parts += [np.tile(np.cos(angle), (1, 2)), np.tile(np.sin(angle), (1, 2))]
+    return np.concatenate(parts).astype(np.float32)
 
 
 def kernel(
-    hid, dest, docs, cos, sin, wq, wk, wv, out,
-    x_all, w_all, dests, pack, unpack, meta_s, meta_r, qkv, snd, rcv, keys, vals, qs, outs, bias,
+    hid, dest, docs, table, wq, wk, wv, out,
+    cos, sin, turn, x_all, w_all, dests, pack, unpack, meta_s, meta_r, qkv, snd, rcv, keys, vals, qs, outs, bias,
     one, six,
 ):
     dp, cx = lax.axis_index("dp"), lax.axis_index("ctx")
@@ -44,8 +54,8 @@
         return lax.rem(chip + step, CHIPS)
 
     (hid_l, hid_s, hid_r, dst_s, dst_r, met_s, met_r) = (one.at[i] for i in range(7))
-    (w_l, w_s, w_r, y_s, y_r, x_s, x_r, z_s, z_r, a_s, a_r, h_s, h_r, o_l, o_s, o_r) = (
-        six.at[i] for i in range(16)
+    (w_l, w_s, w_r, y_s, y_r, x_s, x_r, z_s, z_r, a_s, a_r, h_s, h_r, o_l, o_s, o_r, f_s, f_r) = (
+        six.at[i] for i in range(18)
     )
 
     barrier = pltpu.get_barrier_semaphore()
@@ -72,51 +82,77 @@
     mine = pl.ds(pl.multiple_of(core * 256, 256), 256)
     my_rows = pl.ds(pl.multiple_of(core * BLOCK, BLOCK), BLOCK)
     for k in range(CHUNKS):
-        spot = w_all.at[k, chip, mine]
+        spot = w_all.at[k, 0, mine]
         remote(columns(k, other), spot, w_s.at[k], w_r.at[k], sibling).start()
         pltpu.make_async_copy(columns(k, core), spot, w_l.at[k]).start()
     dests[core] = jnp.broadcast_to(dest[...], (8, BLOCK))
     remote(dests.at[core], dests.at[core], dst_s, dst_r, sibling).start()
-    remote(hid, x_all.at[my_rows], hid_s, hid_r, sibling).start()
-    pltpu.make_async_copy(hid, x_all.at[my_rows], hid_l).start()
-
-    sent_half = pl.ds(pl.multiple_of(half * 256, 256), 256)
-    low = pl.ds(pl.multiple_of(half * 256, 128), 128)
-    high = pl.ds(pl.multiple_of(half * 256 + 128, 128), 128)
+
+    def run(start, size):
+        return pl.ds(pl.multiple_of(start, size), size)
+
+    def part(k, shards):
+        rows = run(z * 128, 128) if QUARTERS[k] else run(half * 256, 256)
+        return w_all.at[k, shards, rows]
+
+    def shape(k, n, rows):
+        return w_all.at[k, pl.ds(0, n), pl.ds(0, rows)]
+
+    def width(k):
+        return 128 if QUARTERS[k] else 256
 
     def stage_y(k):
-        own = w_all.at[k, chip, mine]
+        own = w_all.at[k, 0, mine]
         drain(own, w_l.at[k])
         drain(own, w_r.at[k])
-        spot = w_all.at[k, chip, sent_half]
         for step in (1, 3, 2):
-            remote(spot, spot, y_s.at[k], y_r.at[k], (dp, xl * 8 + at_y(step) * 2 + core)).start()
-        remote(spot, spot, x_s.at[k], x_r.at[k], inner).start()
-
-    def to_z(k, shard):
-        spot = w_all.at[k, shard, low]
-        remote(spot, spot, z_s.at[k], z_r.at[k], below).start()
-        spot = w_all.at[k, shard, high]
-        remote(spot, spot, z_s.at[k], z_r.at[k], above).start()
-
-    def pieces(k, n):
-        return w_all.at[k, pl.ds(0, n), pl.ds(0, 256)]
+            remote(
+                part(k, 0), part(k, 4 - step), y_s.at[k], y_r.at[k],
+                (dp, xl * 8 + at_y(step) * 2 + core),
+            ).start()
+        remote(
+            part(k, 0), part(k, 4), x_s.at[k], x_r.at[k], outer if QUARTERS[k] else inner
+        ).start()
+
+    def to_z(k, shards):
+        for i, device in enumerate((below, above)):
+            if QUARTERS[k]:
+                spot = part(k, shards)
+            else:
+                spot = w_all.at[k, shards, run(half * 256 + i * 128, 128)]
+            remote(spot, spot, z_s.at[k], z_r.at[k], device).start()
 
     def stage_x(k):
-        drain(pieces(k, 3), y_r.at[k])
-        for step in (1, 3, 2):
-            spot = w_all.at[k, xl * 4 + at_y(step), sent_half]
-            remote(spot, spot, x_s.at[k], x_r.at[k], outer).start()
-        for step in (1, 3, 2):
-            to_z(k, xl * 4 + at_y(step))
+        drain(shape(k, 3, width(k)), y_r.at[k])
+        remote(
+            part(k, pl.ds(1, 3)), part(k, pl.ds(5, 3)), x_s.at[k], x_r.at[k], outer
+        ).start()
+        to_z(k, pl.ds(1, 3))
 
     def stage_z(k):
-        drain(pieces(k, 4), x_r.at[k])
-        for step in range(4):
-            to_z(k, (1 - xl) * 4 + at_y(step))
+        drain(shape(k, 4, width(k)), x_r.at[k])
+        to_z(k, pl.ds(4, 4))
+
+    def stage_f(k):
+        if QUARTERS[k]:
+            drain(shape(k, 7, 256), z_r.at[k])
+            spot = w_all.at[k, pl.ds(1, 7), run(lax.rem(z + 3, 4) * 128, 64)]
+            remote(spot, spot, f_s.at[k], f_r.at[k], above).start()
+            spot = w_all.at[k, pl.ds(1, 7), run(lax.rem(z + 1, 4) * 128 + 64, 64)]
+            remote(spot, spot, f_s.at[k], f_r.at[k], below).start()
+
+    def arrived(k):
+        if QUARTERS[k]:
+            drain(shape(k, 7, 128), f_r.at[k])
+        else:
+            drain(shape(k, 7, 256), z_r.at[k])
+
+    def at_step(i, late, stage):
+        for k in range(max(late, 0), CHUNKS):
+            pl.when(i == k - late)(lambda k=k: stage(k))
 
     def project(k):
-        drain(pieces(k, 7), z_r.at[k])
+        at_step(k, 0, arrived)
 
         def rows(m, _):
             at = pl.ds(pl.multiple_of(m * 512, 512), 512)
@@ -228,6 +264,14 @@
 
     stage_y(0)
     stage_y(1)
+    for r in range(CHIPS):
+        shard = (xl if r < 4 else 1 - xl) * 4 + at_y(r % 4)
+        src = hid.at[:, run(shard * 512, 512)]
+        spot = x_all.at[my_rows, pl.ds(r * 512, 512)]
+        remote(src, spot, hid_s, hid_r, sibling).start()
+        pltpu.make_async_copy(src, spot, hid_l).start()
+    for k in range(2, CHUNKS):
+        stage_y(k)
 
     drain(dests.at[core], dst_r)
     tri = (
@@ -276,21 +320,39 @@
     stage_x(0)
 
     def mask(i, _):
-        at = pl.multiple_of(i * 128, 128)
-        own = docs[:, pl.ds(pl.multiple_of(at + 512, 128), 128)].astype(F32)
-        own = jnp.transpose(jnp.broadcast_to(own, (128, 128)))[:, :1]
-        row = lax.broadcasted_iota(jnp.int32, (128, WINDOW), 0)
-        col = lax.broadcasted_iota(jnp.int32, (128, WINDOW), 1)
-        seen = (col > row) & (col <= row + 512)
-        seen = seen & (own == docs[:, pl.ds(at, WINDOW)].astype(F32))
-        bias[i] = jnp.where(seen, 0.0, -1e30)
+        def doc(at):
+            line = docs[pl.ds(jnp.maximum(at, 0), 1), :].astype(F32)
+            return jnp.where(at >= 0, line, -1.0)
+
+        own = jnp.transpose(jnp.broadcast_to(doc(chip * 8 + i), (128, 128)))
+        row = lax.broadcasted_iota(jnp.int32, (128, 128), 0)
+        for j in range(5):
+            col = lax.broadcasted_iota(jnp.int32, (128, 128), 1) + j * 128
+            seen = (col > row) & (col <= row + 512) & (own == doc(chip * 8 - 4 + i + j))
+            bias[i, :, j * 128 : (j + 1) * 128] = jnp.where(seen, 0.0, -1e30)
         return 0
 
     lax.fori_loop(0, 8, mask, 0)
 
-    stage_y(2)
     stage_x(1)
     stage_z(0)
+
+    cc, cs = table[pl.ds(chip, 1), :], table[pl.ds(8 + chip, 1), :]
+    turn[0] = table[16:48, :] * cc - table[48:80, :] * cs
+    turn[1] = table[48:80, :] * cc + table[16:48, :] * cs
+    sign = jnp.where(lax.broadcasted_iota(jnp.int32, (1, HEAD), 1) < 64, -1.0, 1.0)
+
+    def rotary(i, _):
+        at = run(i * 32, 32)
+        ca, sa = turn[0, pl.ds(i, 1), :], turn[1, pl.ds(i, 1), :]
+        cos[at, :] = table[80:112, :] * ca - table[112:144, :] * sa
+        sin[at, :] = (table[112:144, :] * ca + table[80:112, :] * sa) * sign
+        return 0
+
+    lax.fori_loop(0, 32, rotary, 0)
+
+    stage_x(2)
+    stage_z(1)
 
     drain(meta_r.at[pl.ds(0, 7)], met_r)
     place = lax.broadcasted_iota(jnp.int32, (BLOCK, 128), 0).astype(F32) + 1.0
@@ -302,21 +364,13 @@
     drain(x_all.at[my_rows], hid_r)
 
     def step(i, _):
-        @pl.when(i < CHUNKS - 3)
-        def _():
-            stage_y(i + 3)
-
-        @pl.when(i < CHUNKS - 2)
-        def _():
-            stage_x(i + 2)
-
-        @pl.when(i < CHUNKS - 1)
-        def _():
-            stage_z(i + 1)
-
         @pl.when(i < CHUNKS)
         def _():
             project(i)
+
+        at_step(i, 3, stage_x)
+        at_step(i, 2, stage_z)
+        at_step(i, 1, stage_f)
 
         @pl.when(i >= 1)
         def _():
@@ -332,10 +386,12 @@
         drain(spot, o_r.at[c])
         drain(outs.at[0, c], o_s.at[c])
     for k in range(CHUNKS):
-        drain(pieces(k, 1), w_s.at[k])
-        drain(pieces(k, 3), y_s.at[k])
-        drain(pieces(k, 4), x_s.at[k])
-        drain(pieces(k, 7), z_s.at[k])
+        drain(shape(k, 1, 256), w_s.at[k])
+        drain(shape(k, 3, width(k)), y_s.at[k])
+        drain(shape(k, 4, width(k)), x_s.at[k])
+        drain(shape(k, 7, 256), z_s.at[k])
+        if QUARTERS[k]:
+            drain(shape(k, 7, 128), f_s.at[k])
         drain(snd.at[k, pl.ds(0, 7)], a_s.at[k])
     drain(keys.at[:, pl.ds(0, 512)], h_s.at[0])
     drain(vals.at[:, pl.ds(0, 512)], h_s.at[1])
@@ -345,24 +401,17 @@
 
 
 def on_device(hidden, dest, doc_ids, w_query, key_weight, value_weight):
-    chip = lax.axis_index("ctx") // 2
-    positions = (chip * 1024 + jnp.arange(1024, dtype=jnp.int32)).astype(F32)
-    freq = jnp.arange(HEAD // 2, dtype=F32)
-    inverse = jnp.exp(-(2.0 * freq / HEAD) * jnp.log(F32(rope_base)))
-    angles = positions[:, None] * inverse[None, :]
-    cosine, sine = jnp.cos(angles), jnp.sin(angles)
-    cosine = jnp.concatenate([cosine, cosine], axis=1)
-    sine = jnp.concatenate([-sine, sine], axis=1)
-    docs = jnp.concatenate([jnp.full((BLOCK,), -1, jnp.int32), doc_ids])
-    docs = lax.dynamic_slice_in_dim(docs, chip * 1024, 1536, 0).reshape(1, 1536)
     anywhere = pl.BlockSpec(memory_space=pl.ANY)
     local = pl.BlockSpec(memory_space=pltpu.VMEM)
     return pl.pallas_call(
         kernel,
         out_shape=jax.ShapeDtypeStruct((BLOCK, 2048), BF16),
-        in_specs=[anywhere, local, local, local, local, anywhere, anywhere, anywhere],
+        in_specs=[anywhere, local, local, local, anywhere, anywhere, anywhere],
         out_specs=anywhere,
         scratch_shapes=[
+            pltpu.VMEM((1024, HEAD), F32),
+            pltpu.VMEM((1024, HEAD), F32),
+            pltpu.VMEM((2, 32, HEAD), F32),
             pltpu.VMEM((1024, 4096), BF16),
             pltpu.VMEM((CHUNKS, CHIPS, 512, WIDE), BF16),
             pltpu.VMEM((2, 8, BLOCK), jnp.int32),
@@ -379,12 +428,15 @@
             pltpu.VMEM((2, 4, BLOCK, WIDE), BF16),
             pltpu.VMEM((8, 128, WINDOW), F32),
             pltpu.SemaphoreType.DMA((7,)),
-            pltpu.SemaphoreType.DMA((16, CHUNKS)),
+            pltpu.SemaphoreType.DMA((18, CHUNKS)),
         ],
         compiler_params=pltpu.CompilerParams(
             collective_id=0, has_side_effects=True, vmem_limit_bytes=60 * 2**20
         ),
-    )(hidden, dest.reshape(1, BLOCK), docs, cosine, sine, w_query, key_weight, value_weight)
+    )(
+        hidden, dest.reshape(1, BLOCK), doc_ids.reshape(64, 128), jnp.asarray(angles()),
+        w_query, key_weight, value_weight,
+    )
 
 
 def solution(mesh):

time: 160 us -> 147 us (0.919)
  the two profiles are of different devices: /device:TPU:123 before, /device:TPU:26 now
where the time goes in v1:
time: 147 us; the launch traced here: 146 us
  Pallas kernels  143 us (97%)
  local copies, waits for them, and re-layouts  3.16 us (2%)
    pallas_call x1, Pallas kernels, on_device(): pl.pallas_call(kernel, out_shape=jax.ShapeDtypeStruct((BLOCK, 2048), BF16...  143 us
    unnamed x1, local copies, waits for them, and re-layouts  3.16 us

profile of v1, /device:TPU:26, one launch (start us, length us, event | category | flops | bytes accessed | tf_op | source)
XLA Modules:
  0.0 145.7 jit_solution(6004785607788025814)
XLA Ops:
  0.0 142.5 %shard_map.73 = bf16[512,2048]{1,0:T(8,128)(2,1)} custom-call(bf16[512,4096]{1,0:T(8,128)(2,1)} %hid.1, s32[1,512]{1,0:T(1,128)} %bitcast.3, s32[64,128]{1,0:T(8,128)} %bitcast.2, f32[144,128]{1,0:T(8,128)} %constant.2.clone.table, bf16[256,2048]{1,0:T(8,128)(2,1)} %wq.1, bf16[256,512]{1,0:T(8,128)(2,1)} %wk.1, bf16[256,512]{1,0:T(8,128)(2,1)} %wv.1), custom_call_target="tpu_custom_call" | custom-call | tf_op jit(solution)/shard_map/pallas_call | solution.py:406
  142.5 3.2 %copy.9 = bf16[512,2048]{1,0:T(8,128)(2,1)} copy(bf16[512,2048]{1,0:T(8,128)(2,1)} %shard_map.73) | data formatting | bytes 4194304

commit v2 on v1

--- a/solution.py
+++ b/solution.py
@@ -17,7 +17,7 @@
 rope_base = 500000.0 * 16.0 ** (128.0 / 126.0)
 SCORE = HEAD**-0.5 * 1.4426950408889634
 F32, BF16 = jnp.float32, jnp.bfloat16
-QUARTERS = (False, False, True, True, True, True)
+QUARTERS = (False, False, False, False, True, True)
 
 
 def angles():
@@ -239,7 +239,8 @@
     def attend(c):
         g = c // 2
 
-        def tile(i, _):
+        def tile(n, _):
+            i = lax.rem(n + other * 4, 8)
             at = pl.multiple_of(i * 128, 128)
             q = qs[:, pl.ds(at, 128), :].reshape(256, HEAD)
             s = lax.dot_general(
@@ -257,21 +258,22 @@
             outs[i // 4, c, to, pl.ds(HEAD, HEAD)] = o[128:]
             return 0
 
-        lax.fori_loop(0, 8, tile, 0)
+        lax.fori_loop(0, 4, tile, 0)
         spot = out.at[:, pl.ds(pl.multiple_of(core * 1024 + c * WIDE, WIDE), WIDE)]
         remote(outs.at[other, c], spot, o_s.at[c], o_r.at[c], sibling).start()
+        lax.fori_loop(4, 8, tile, 0)
         pltpu.make_async_copy(outs.at[core, c], spot, o_l.at[c]).start()
 
     stage_y(0)
     stage_y(1)
+    stage_y(2)
+    stage_y(3)
     for r in range(CHIPS):
         shard = (xl if r < 4 else 1 - xl) * 4 + at_y(r % 4)
         src = hid.at[:, run(shard * 512, 512)]
         spot = x_all.at[my_rows, pl.ds(r * 512, 512)]
         remote(src, spot, hid_s, hid_r, sibling).start()
         pltpu.make_async_copy(src, spot, hid_l).start()
-    for k in range(2, CHUNKS):
-        stage_y(k)
 
     drain(dests.at[core], dst_r)
     tri = (
@@ -318,6 +320,7 @@
     meta_r[chip] = meta_s[chip]
 
     stage_x(0)
+    stage_y(4)
 
     def mask(i, _):
         def doc(at):
@@ -335,6 +338,7 @@
     lax.fori_loop(0, 8, mask, 0)
 
     stage_x(1)
+    stage_y(5)
     stage_z(0)
 
     cc, cs = table[pl.ds(chip, 1), :], table[pl.ds(8 + chip, 1), :]
@@ -405,9 +409,9 @@
     local = pl.BlockSpec(memory_space=pltpu.VMEM)
     return pl.pallas_call(
         kernel,
-        out_shape=jax.ShapeDtypeStruct((BLOCK, 2048), BF16),
+        out_shape=pltpu.VMEM((BLOCK, 2048), BF16),
         in_specs=[anywhere, local, local, local, anywhere, anywhere, anywhere],
-        out_specs=anywhere,
+        out_specs=local,
         scratch_shapes=[
             pltpu.VMEM((1024, HEAD), F32),
             pltpu.VMEM((1024, HEAD), F32),

time: 147 us -> 136 us (0.925)
  Pallas kernels: 143 us -> 134 us
  local copies, waits for them, and re-layouts: 3.16 us -> 1.32 us
    pallas_call x1, Pallas kernels: 143 us -> 134 us  [on_device(): pl.pallas_call(kernel, out_shape=pltpu.VMEM((BLOCK, 2048), BF16), in_spec...]
    unnamed x1, local copies, waits for them, and re-layouts: 3.16 us -> 1.32 us
where the time goes in v2:
time: 136 us
  Pallas kernels  134 us (99%)
    pallas_call x1, Pallas kernels, on_device(): pl.pallas_call(kernel, out_shape=pltpu.VMEM((BLOCK, 2048), BF16), in_spec...  134 us

profile of v2, /device:TPU:26, one launch (start us, length us, event | category | flops | bytes accessed | tf_op | source)
XLA Modules:
  0.0 135.5 jit_solution(4207317381295118180)
XLA Ops:
  0.0 134.2 %shard_map.73 = bf16[512,2048]{1,0:T(8,128)(2,1)S(1)} custom-call(bf16[512,4096]{1,0:T(8,128)(2,1)} %hid.1, s32[1,512]{1,0:T(1,128)} %bitcast.3, s32[64,128]{1,0:T(8,128)} %bitcast.2, f32[144,128]{1,0:T(8,128)} %constant.2.clone.table, bf16[256,2048]{1,0:T(8,128)(2,1)} %wq.1, bf16[256,512]{1,0:T(8,128)(2,1)} %wk.1, bf16[256,512]{1,0:T(8,128)(2,1)} %wv.1), custom_call_target="tpu_custom_call" | custom-call | tf_op jit(solution)/shard_map/pallas_call | solution.py:410
  134.2 1.3 copy.9

commit v3 on v2

--- a/solution.py
+++ b/solution.py
@@ -81,10 +81,12 @@
 
     mine = pl.ds(pl.multiple_of(core * 256, 256), 256)
     my_rows = pl.ds(pl.multiple_of(core * BLOCK, BLOCK), BLOCK)
-    for k in range(CHUNKS):
+    def shard_in(k):
         spot = w_all.at[k, 0, mine]
         remote(columns(k, other), spot, w_s.at[k], w_r.at[k], sibling).start()
         pltpu.make_async_copy(columns(k, core), spot, w_l.at[k]).start()
+
+    shard_in(0)
     dests[core] = jnp.broadcast_to(dest[...], (8, BLOCK))
     remote(dests.at[core], dests.at[core], dst_s, dst_r, sibling).start()
 
@@ -124,9 +126,12 @@
 
     def stage_x(k):
         drain(shape(k, 3, width(k)), y_r.at[k])
-        remote(
-            part(k, pl.ds(1, 3)), part(k, pl.ds(5, 3)), x_s.at[k], x_r.at[k], outer
-        ).start()
+        moves = ((1, 1, inner), (2, 2, outer)) if k in (0,) else ((1, 3, outer),)
+        for first, count, device in moves:
+            remote(
+                part(k, pl.ds(first, count)), part(k, pl.ds(4 + first, count)),
+                x_s.at[k], x_r.at[k], device,
+            ).start()
         to_z(k, pl.ds(1, 3))
 
     def stage_z(k):
@@ -258,23 +263,18 @@
             outs[i // 4, c, to, pl.ds(HEAD, HEAD)] = o[128:]
             return 0
 
-        lax.fori_loop(0, 4, tile, 0)
+        lax.fori_loop(0, 4, tile, 0, unroll=4)
         spot = out.at[:, pl.ds(pl.multiple_of(core * 1024 + c * WIDE, WIDE), WIDE)]
         remote(outs.at[other, c], spot, o_s.at[c], o_r.at[c], sibling).start()
-        lax.fori_loop(4, 8, tile, 0)
+        lax.fori_loop(4, 8, tile, 0, unroll=4)
         pltpu.make_async_copy(outs.at[core, c], spot, o_l.at[c]).start()
 
     stage_y(0)
+    for k in range(1, CHUNKS):
+        shard_in(k)
     stage_y(1)
     stage_y(2)
     stage_y(3)
-    for r in range(CHIPS):
-        shard = (xl if r < 4 else 1 - xl) * 4 + at_y(r % 4)
-        src = hid.at[:, run(shard * 512, 512)]
-        spot = x_all.at[my_rows, pl.ds(r * 512, 512)]
-        remote(src, spot, hid_s, hid_r, sibling).start()
-        pltpu.make_async_copy(src, spot, hid_l).start()
-
     drain(dests.at[core], dst_r)
     tri = (
         lax.broadcasted_iota(jnp.int32, (BLOCK, BLOCK), 0)
@@ -321,6 +321,13 @@
 
     stage_x(0)
     stage_y(4)
+
+    for r in range(CHIPS):
+        shard = (xl if r < 4 else 1 - xl) * 4 + at_y(r % 4)
+        src = hid.at[:, run(shard * 512, 512)]
+        spot = x_all.at[my_rows, pl.ds(r * 512, 512)]
+        remote(src, spot, hid_s, hid_r, sibling).start()
+        pltpu.make_async_copy(src, spot, hid_l).start()
 
     def mask(i, _):
         def doc(at):

time: 136 us -> 132 us (0.971)
  Pallas kernels: 134 us -> 130 us
    pallas_call x1, Pallas kernels: 134 us -> 130 us  [on_device(): pl.pallas_call(kernel, out_shape=pltpu.VMEM((BLOCK, 2048), BF16), in_spec...]
where the time goes in v3:
time: 132 us; the launch traced here: 131 us
  Pallas kernels  130 us (98%)
  local copies, waits for them, and re-layouts  1.32 us (1%)
    pallas_call x1, Pallas kernels, on_device(): pl.pallas_call(kernel, out_shape=pltpu.VMEM((BLOCK, 2048), BF16), in_spec...  130 us

profile of v3, /device:TPU:26, one launch (start us, length us, event | category | flops | bytes accessed | tf_op | source)
XLA Modules:
  0.0 131.2 jit_solution(16941094483598785896)
XLA Ops:
  0.0 129.9 %shard_map.73 = bf16[512,2048]{1,0:T(8,128)(2,1)S(1)} custom-call(bf16[512,4096]{1,0:T(8,128)(2,1)} %hid.1, s32[1,512]{1,0:T(1,128)} %bitcast.3, s32[64,128]{1,0:T(8,128)} %bitcast.2, f32[144,128]{1,0:T(8,128)} %constant.2.clone.table, bf16[256,2048]{1,0:T(8,128)(2,1)} %wq.1, bf16[256,512]{1,0:T(8,128)(2,1)} %wk.1, bf16[256,512]{1,0:T(8,128)(2,1)} %wv.1), custom_call_target="tpu_custom_call" | custom-call | tf_op jit(solution)/shard_map/pallas_call | solution.py:417
  129.9 1.3 %copy.9 = bf16[512,2048]{1,0:T(8,128)(2,1)} copy(bf16[512,2048]{1,0:T(8,128)(2,1)S(1)} %shard_map.73) | data formatting | bytes 4194304

commit v4 on v3

--- a/solution.py
+++ b/solution.py
@@ -17,6 +17,7 @@
 rope_base = 500000.0 * 16.0 ** (128.0 / 126.0)
 SCORE = HEAD**-0.5 * 1.4426950408889634
 F32, BF16 = jnp.float32, jnp.bfloat16
+BOTH = (0, 5)
 QUARTERS = (False, False, False, False, True, True)
 
 
@@ -113,7 +114,7 @@
                 (dp, xl * 8 + at_y(step) * 2 + core),
             ).start()
         remote(
-            part(k, 0), part(k, 4), x_s.at[k], x_r.at[k], outer if QUARTERS[k] else inner
+            part(k, 0), part(k, 4), x_s.at[k], x_r.at[k], outer if QUARTERS[k] and k not in BOTH else inner
         ).start()
 
     def to_z(k, shards):
@@ -126,7 +127,7 @@
 
     def stage_x(k):
         drain(shape(k, 3, width(k)), y_r.at[k])
-        moves = ((1, 1, inner), (2, 2, outer)) if k in (0,) else ((1, 3, outer),)
+        moves = ((1, 1, inner), (2, 2, outer)) if k in BOTH else ((1, 3, outer),)
         for first, count, device in moves:
             remote(
                 part(k, pl.ds(first, count)), part(k, pl.ds(4 + first, count)),
@@ -379,9 +380,9 @@
         def _():
             project(i)
 
+        at_step(i, 1, stage_f)
+        at_step(i, 2, stage_z)
         at_step(i, 3, stage_x)
-        at_step(i, 2, stage_z)
-        at_step(i, 1, stage_f)
 
         @pl.when(i >= 1)
         def _():

time: 132 us -> 131 us (level)
  Pallas kernels: 130 us -> 128 us
    pallas_call x1, Pallas kernels: 130 us -> 128 us  [on_device(): pl.pallas_call(kernel, out_shape=pltpu.VMEM((BLOCK, 2048), BF16), in_spec...]
where the time goes in v4:
time: 131 us; the launch traced here: 130 us
  Pallas kernels  128 us (98%)
  local copies, waits for them, and re-layouts  1.32 us (1%)
    pallas_call x1, Pallas kernels, on_device(): pl.pallas_call(kernel, out_shape=pltpu.VMEM((BLOCK, 2048), BF16), in_spec...  128 us

profile of v4, /device:TPU:26, one launch (start us, length us, event | category | flops | bytes accessed | tf_op | source)
XLA Modules:
  0.0 129.6 jit_solution(11290727307409195791)
XLA Ops:
  0.0 128.2 %shard_map.73 = bf16[512,2048]{1,0:T(8,128)(2,1)S(1)} custom-call(bf16[512,4096]{1,0:T(8,128)(2,1)} %hid.1, s32[1,512]{1,0:T(1,128)} %bitcast.3, s32[64,128]{1,0:T(8,128)} %bitcast.2, f32[144,128]{1,0:T(8,128)} %constant.2.clone.table, bf16[256,2048]{1,0:T(8,128)(2,1)} %wq.1, bf16[256,512]{1,0:T(8,128)(2,1)} %wk.1, bf16[256,512]{1,0:T(8,128)(2,1)} %wv.1), custom_call_target="tpu_custom_call" | custom-call | tf_op jit(solution)/shard_map/pallas_call | solution.py:418
  128.2 1.3 %copy.9 = bf16[512,2048]{1,0:T(8,128)(2,1)} copy(bf16[512,2048]{1,0:T(8,128)(2,1)S(1)} %shard_map.73) | data formatting | bytes 4194304

commit v5 on v3

--- a/solution.py
+++ b/solution.py
@@ -113,7 +113,7 @@
                 (dp, xl * 8 + at_y(step) * 2 + core),
             ).start()
         remote(
-            part(k, 0), part(k, 4), x_s.at[k], x_r.at[k], outer if QUARTERS[k] else inner
+            part(k, 0), part(k, 4), x_s.at[k], x_r.at[k], outer if QUARTERS[k] and k != 5 else inner
         ).start()
 
     def to_z(k, shards):
@@ -126,7 +126,7 @@
 
     def stage_x(k):
         drain(shape(k, 3, width(k)), y_r.at[k])
-        moves = ((1, 1, inner), (2, 2, outer)) if k in (0,) else ((1, 3, outer),)
+        moves = ((1, 1, inner), (2, 2, outer)) if k in (0, 5) else ((1, 3, outer),)
         for first, count, device in moves:
             remote(
                 part(k, pl.ds(first, count)), part(k, pl.ds(4 + first, count)),

time: 132 us -> 131 us (level)
  no operation moved by 1% of the time
where the time goes in v5:
time: 131 us; the launch traced here: 130 us
  Pallas kernels  129 us (98%)
  local copies, waits for them, and re-layouts  1.32 us (1%)
    pallas_call x1, Pallas kernels, on_device(): pl.pallas_call(kernel, out_shape=pltpu.VMEM((BLOCK, 2048), BF16), in_spec...  129 us

profile of v5, /device:TPU:26, one launch (start us, length us, event | category | flops | bytes accessed | tf_op | source)
XLA Modules:
  0.0 130.1 jit_solution(9955303723537316423)
XLA Ops:
  0.0 128.8 %shard_map.73 = bf16[512,2048]{1,0:T(8,128)(2,1)S(1)} custom-call(bf16[512,4096]{1,0:T(8,128)(2,1)} %hid.1, s32[1,512]{1,0:T(1,128)} %bitcast.3, s32[64,128]{1,0:T(8,128)} %bitcast.2, f32[144,128]{1,0:T(8,128)} %constant.2.clone.table, bf16[256,2048]{1,0:T(8,128)(2,1)} %wq.1, bf16[256,512]{1,0:T(8,128)(2,1)} %wk.1, bf16[256,512]{1,0:T(8,128)(2,1)} %wv.1), custom_call_target="tpu_custom_call" | custom-call | tf_op jit(solution)/shard_map/pallas_call | solution.py:417
  128.8 1.3 %copy.9 = bf16[512,2048]{1,0:T(8,128)(2,1)} copy(bf16[512,2048]{1,0:T(8,128)(2,1)S(1)} %shard_map.73) | data formatting | bytes 4194304
